TPU v7x, 32 devices: a whole 2x2x4 slice. The times are simulated.
32 devices in a mesh: dp: 8 (over z, x), tensor: 4 (over y, core).
Axes of the slice: x: 2, y: 2, z: 4, core: 2. Of those that a mesh axis runs over, the one named last changes fastest.
Arguments:
- tokens: bfloat16 [10976, 1280], P(('dp', 'tensor')), may hold values from -6 to 6
- grad_out: bfloat16 [10976, 1280], P(('dp', 'tensor')), may hold values from -6 to 6
- adapter_index: int32 [2], replicated, may hold values from 0 to 7
- norm1_gain: bfloat16 [1280], replicated, may hold values from 0.099609375 to 1.8984375
- norm1_shift: bfloat16 [1280], replicated, may hold values from -2.5 to 2.5
- qkv_weight: bfloat16 [1280, 3, 1280], P(None, None, 'tensor'), may hold values from -0.15625 to 0.15625
- qkv_bias: bfloat16 [3, 1280], P(None, 'tensor'), may hold values from -2.5 to 2.5
- rel_pos_h: bfloat16 [27, 80], replicated, may hold values from -1.25 to 1.25
- rel_pos_w: bfloat16 [27, 80], replicated, may hold values from -1.25 to 1.25
- proj_weight: bfloat16 [1280, 1280], P('tensor'), may hold values from -0.625 to 0.625
- proj_bias: bfloat16 [1280], replicated, may hold values from -2.5 to 2.5
- norm2_gain: bfloat16 [1280], replicated, may hold values from 0.099609375 to 1.8984375
- norm2_shift: bfloat16 [1280], replicated, may hold values from -2.5 to 2.5
- lin1_weight: bfloat16 [1280, 5120], P(None, 'tensor'), may hold values from -0.15625 to 0.15625
- lin1_bias: bfloat16 [5120], P('tensor'), may hold values from -2.5 to 2.5
- lin2_weight: bfloat16 [5120, 1280], P('tensor'), may hold values from -0.078125 to 0.078125
- lin2_bias: bfloat16 [1280], replicated, may hold values from -2.5 to 2.5
- qkv_down: bfloat16 [8, 1280, 16], replicated, may hold values from -0.15625 to 0.15625
- qkv_up: bfloat16 [8, 16, 3, 1280], P(None, None, None, 'tensor'), may hold values from -1.5 to 1.5
- proj_down: bfloat16 [8, 1280, 16], P(None, 'tensor'), may hold values from -0.625 to 0.625
- proj_up: bfloat16 [8, 16, 1280], replicated, may hold values from -1.5 to 1.5
- lin1_down: bfloat16 [8, 1280, 16], replicated, may hold values from -0.15625 to 0.15625
- lin1_up: bfloat16 [8, 16, 5120], P(None, None, 'tensor'), may hold values from -1.5 to 1.5
- lin2_down: bfloat16 [8, 5120, 16], P(None, 'tensor'), may hold values from -0.078125 to 0.078125
- lin2_up: bfloat16 [8, 16, 1280], replicated, may hold values from -1.5 to 1.5
Outputs:
- output: bfloat16 [10976, 1280], P(('dp', 'tensor'))
- grad_tokens: bfloat16 [10976, 1280], P(('dp', 'tensor'))
- grad_qkv_down: float32 [8, 1280, 16], replicated
- grad_qkv_up: float32 [8, 16, 3, 1280], P(None, None, None, 'tensor')
- grad_proj_down: float32 [8, 1280, 16], P(None, 'tensor')
- grad_proj_up: float32 [8, 16, 1280], replicated
- grad_lin1_down: float32 [8, 1280, 16], replicated
- grad_lin1_up: float32 [8, 16, 5120], P(None, None, 'tensor')
- grad_lin2_down: float32 [8, 5120, 16], P(None, 'tensor')
- grad_lin2_up: float32 [8, 16, 1280], replicated
Inputs may be any that keep to these rules, and one draw needn't show every extreme that they name: `adapter_index`: one adapter for each image.
All inputs are finite; a program needn't handle non-finite values.
Results may differ from a plain program's by a relative error of at most 0.019.
Values may be sent and summed in bfloat16 or wider, within the bound.
A program may use at most 256 MiB of HBM per device.

v0:
```python
import jax
import jax.numpy as jnp
from jax import lax
from jax.sharding import PartitionSpec as P

HEAD_DIM = 80
WIN = 14
SIDE = 64
RANK = 16
ADAPTERS = 8
WIN_DEV = 7
GROUP = 4
GRID = 5
HIGH = lax.Precision.HIGHEST
ADAPT = 0.5
EPS = 1e-06


def fast_dot(first_op, second_op):
    return jnp.dot(first_op, second_op, preferred_element_type=jnp.float32)


def trans_dot(first_op, second_op):
    return lax.dot_general(
        first_op, second_op, (((1,), (1,)), ((), ())), preferred_element_type=jnp.float32
    )


def exact_dot(first_op, second_op):
    return jnp.dot(first_op, second_op.astype(jnp.float32), precision=HIGH)


def cross_dot(first_op, second_op):
    return lax.dot_general(
        first_op.astype(jnp.float32),
        second_op.astype(jnp.float32),
        (((0,), (0,)), ((), ())),
        precision=HIGH,
    )


def window_mask(first_slot, count_all):
    position = jnp.arange(count_all, dtype=jnp.int32)
    slot_index = first_slot + position // (WIN * WIN)
    within = position % (WIN * WIN)
    image_row = slot_index // GRID * WIN + within // WIN
    image_col = slot_index % GRID * WIN + within % WIN
    inside = (slot_index < GRID * GRID) & (image_row < SIDE) & (image_col < SIDE)
    return jnp.where(inside, 1.0, 0.0).astype(jnp.float32)[:, None]


def offset_table(position_table):
    offsets = (jnp.arange(WIN)[:, None] - jnp.arange(WIN)[None, :] + WIN - 1).reshape(-1)
    one_hot = (offsets[:, None] == jnp.arange(2 * WIN - 1)[None, :]).astype(jnp.float32)
    return exact_dot(one_hot, position_table).reshape(WIN, WIN, -1).astype(jnp.bfloat16)


def norm_parts(values):
    row_mean = jnp.mean(values, axis=-1, keepdims=True)
    centered = values - row_mean
    inv_std = lax.rsqrt(jnp.mean(centered * centered, axis=-1, keepdims=True) + EPS)
    return (centered * inv_std, inv_std)


def norm_back(grad_in, normalized, inv_std, norm_gain):
    scaled = grad_in * norm_gain
    return inv_std * (
        scaled
        - jnp.mean(scaled, axis=-1, keepdims=True)
        - normalized * jnp.mean(scaled * normalized, axis=-1, keepdims=True)
    )


def window_scores(queries, key_win, table_h, table_w):
    win_count, head_count = (queries.shape[0], queries.shape[1])
    tokens_win = WIN * WIN
    base_scores = jnp.einsum(
        "nhqc,nhkc->nhqk",
        queries.reshape(win_count, head_count, tokens_win, -1),
        key_win.reshape(win_count, head_count, tokens_win, -1),
        preferred_element_type=jnp.float32,
    ) * HEAD_DIM ** (-0.5)
    rel_rows = jnp.einsum("nhabc,akc->nhabk", queries, table_h, preferred_element_type=jnp.float32)
    rel_cols = jnp.einsum("nhabc,bkc->nhabk", queries, table_w, preferred_element_type=jnp.float32)
    scores = (
        base_scores.reshape(win_count, head_count, WIN, WIN, WIN, WIN)
        + rel_rows[:, :, :, :, :, None]
        + rel_cols[:, :, :, :, None, :]
    )
    return scores.reshape(win_count, head_count, tokens_win, tokens_win)


def attention_back(queries, key_win, value_win, log_total, grad_att, table_h, table_w):
    win_count, head_count = (queries.shape[0], queries.shape[1])
    tokens_win = WIN * WIN
    probs = jnp.exp(window_scores(queries, key_win, table_h, table_w) - log_total)
    grad_rows = grad_att.reshape(win_count, head_count, tokens_win, -1)
    dprob = jnp.einsum(
        "nhqc,nhkc->nhqk",
        grad_rows,
        value_win.reshape(win_count, head_count, tokens_win, -1),
        preferred_element_type=jnp.float32,
    )
    dvalues = jnp.einsum(
        "nhqk,nhqc->nhkc", probs.astype(jnp.bfloat16), grad_rows, preferred_element_type=jnp.float32
    )
    inner_sum = jnp.sum(probs * dprob, axis=-1, keepdims=True)
    dscore = (probs * (dprob - inner_sum)).astype(jnp.bfloat16)
    dqueries = jnp.einsum(
        "nhqk,nhkc->nhqc",
        dscore,
        key_win.reshape(win_count, head_count, tokens_win, -1),
        preferred_element_type=jnp.float32,
    ) * HEAD_DIM ** (-0.5)
    dkeys = jnp.einsum(
        "nhqk,nhqc->nhkc",
        dscore,
        queries.reshape(win_count, head_count, tokens_win, -1),
        preferred_element_type=jnp.float32,
    ) * HEAD_DIM ** (-0.5)
    dscore_six = dscore.astype(jnp.float32).reshape(win_count, head_count, WIN, WIN, WIN, WIN)
    from_rows = jnp.einsum(
        "nhabk,akc->nhabc", jnp.sum(dscore_six, axis=5), table_h.astype(jnp.float32), precision=HIGH
    )
    from_cols = jnp.einsum(
        "nhabk,bkc->nhabc", jnp.sum(dscore_six, axis=4), table_w.astype(jnp.float32), precision=HIGH
    )
    dqueries = dqueries.reshape(queries.shape) + from_rows + from_cols
    return (
        dqueries.astype(jnp.bfloat16),
        dkeys.reshape(queries.shape).astype(jnp.bfloat16),
        dvalues.reshape(queries.shape).astype(jnp.bfloat16),
    )


def on_device(
    tokens,
    grad_out,
    adapter_index,
    norm1_gain,
    norm1_shift,
    qkv_weight,
    qkv_bias,
    rel_pos_h,
    rel_pos_w,
    proj_weight,
    proj_bias,
    norm2_gain,
    norm2_shift,
    lin1_weight,
    lin1_bias,
    lin2_weight,
    lin2_bias,
    qkv_down,
    qkv_up,
    proj_down,
    proj_up,
    lin1_down,
    lin1_up,
    lin2_down,
    lin2_up,
):
    tensor_size = lax.axis_size("tensor")
    row_count = tokens.shape[0]
    full_rows = row_count * tensor_size
    dp_place = lax.axis_index("dp")
    tensor_place = lax.axis_index("tensor")
    valid_full = window_mask(dp_place % GROUP * WIN_DEV, full_rows)
    valid_local = lax.dynamic_slice_in_dim(valid_full, tensor_place * row_count, row_count, 0)
    image_place = dp_place // GROUP
    pick = jnp.sum(jnp.where(jnp.arange(adapter_index.shape[0]) == image_place, adapter_index, 0))
    slot_hot = jnp.where(jnp.arange(ADAPTERS) == pick, 1.0, 0.0).astype(jnp.float32)

    def select(table_all):
        return lax.dynamic_index_in_dim(table_all, pick, 0, keepdims=False)

    def into_slot(term):
        return slot_hot.reshape((-1,) + (1,) * term.ndim) * term[None]

    head_local = qkv_weight.shape[2] // HEAD_DIM
    width_local = qkv_weight.shape[2]

    def to_windows(values):
        return values.reshape(-1, WIN, WIN, head_local, HEAD_DIM).transpose(0, 3, 1, 2, 4)

    def from_windows(values):
        return values.transpose(0, 2, 3, 1, 4).reshape(full_rows, -1)

    gain_one = norm1_gain.astype(jnp.float32)
    gain_two = norm2_gain.astype(jnp.float32)
    table_h = offset_table(rel_pos_h)
    table_w = offset_table(rel_pos_w)
    a_qkv = select(qkv_down)
    b_qkv = select(qkv_up).reshape(RANK, -1)
    a_proj = select(proj_down)
    b_proj = select(proj_up)
    a_lin1 = select(lin1_down)
    b_lin2 = select(lin2_up)
    qkv_flat = qkv_weight.reshape(qkv_weight.shape[0], -1)
    x_local = tokens.astype(jnp.float32)
    normal_one, inv_one = norm_parts(x_local)
    xn1_local = (valid_local * (normal_one * gain_one + norm1_shift.astype(jnp.float32))).astype(
        jnp.bfloat16
    )
    xn1 = lax.all_gather(xn1_local, "tensor", axis=0, tiled=True)
    down_q = fast_dot(xn1, a_qkv)
    qkv = (
        fast_dot(xn1, qkv_flat)
        + qkv_bias.astype(jnp.float32).reshape(-1)
        + ADAPT * exact_dot(down_q, b_qkv)
    )
    qkv = qkv.astype(jnp.bfloat16).reshape(full_rows, 3, width_local)
    queries = to_windows(qkv[:, 0])
    key_win = to_windows(qkv[:, 1])
    value_win = to_windows(qkv[:, 2])
    win_count = queries.shape[0]
    tokens_win = WIN * WIN
    scores = window_scores(queries, key_win, table_h, table_w)
    row_max = jnp.max(scores, axis=-1, keepdims=True)
    exponent = jnp.exp(scores - row_max)
    row_total = jnp.sum(exponent, axis=-1, keepdims=True)
    log_total = row_max + jnp.log(row_total)
    probs = exponent / row_total
    attended = jnp.einsum(
        "nhqk,nhkc->nhqc",
        probs.astype(jnp.bfloat16),
        value_win.reshape(win_count, head_local, tokens_win, -1),
        preferred_element_type=jnp.float32,
    )
    att = from_windows(attended.reshape(queries.shape)).astype(jnp.bfloat16)
    down_p = fast_dot(att, a_proj)
    down_part = down_p
    branch_a = lax.psum_scatter(
        (fast_dot(att, proj_weight) + ADAPT * exact_dot(down_part, b_proj)).astype(jnp.bfloat16),
        "tensor",
        scatter_dimension=0,
        tiled=True,
    ).astype(jnp.float32)
    middle = x_local + valid_local * (branch_a + proj_bias.astype(jnp.float32))
    normal_two, inv_two = norm_parts(middle)
    xn2_local = (normal_two * gain_two + norm2_shift.astype(jnp.float32)).astype(jnp.bfloat16)
    xn2 = lax.all_gather(xn2_local, "tensor", axis=0, tiled=True)
    w_lin1, c_lin1, b_lin1, a_lin2, w_lin2 = (
        lin1_weight,
        lin1_bias,
        select(lin1_up),
        select(lin2_down),
        lin2_weight,
    )
    down_1 = fast_dot(xn2, a_lin1)
    hidden_pre = (
        fast_dot(xn2, w_lin1) + c_lin1.astype(jnp.float32) + ADAPT * exact_dot(down_1, b_lin1)
    )
    gelu_value, gelu_grad = jax.vjp(
        lambda values: jax.nn.gelu(values, approximate=False), hidden_pre
    )
    hidden_act = gelu_value.astype(jnp.bfloat16)
    down_2 = fast_dot(hidden_act, a_lin2)
    down_part = down_2
    branch_m = lax.psum_scatter(
        (fast_dot(hidden_act, w_lin2) + ADAPT * exact_dot(down_part, b_lin2)).astype(jnp.bfloat16),
        "tensor",
        scatter_dimension=0,
        tiled=True,
    ).astype(jnp.float32)
    output = (middle + valid_local * (branch_m + lin2_bias.astype(jnp.float32))).astype(
        jnp.bfloat16
    )
    dout_f = grad_out.astype(jnp.float32)
    dy2_local = (valid_local * dout_f).astype(jnp.bfloat16)
    dy2 = lax.all_gather(dy2_local, "tensor", axis=0, tiled=True)
    up2 = trans_dot(dy2, b_lin2)
    dact = trans_dot(dy2, w_lin2) + ADAPT * exact_dot(up2, a_lin2.T)
    dpre = gelu_grad(dact)[0].astype(jnp.bfloat16)
    up1 = trans_dot(dpre, b_lin1)
    grad_lin2_up_t = ADAPT * cross_dot(down_2, dy2)
    grad_lin2_down_t = ADAPT * cross_dot(hidden_act, up2)
    grad_lin1_up_t = ADAPT * cross_dot(down_1, dpre)
    grad_lin1_down_t = ADAPT * cross_dot(xn2, up1)
    up_part = up1
    dxn2 = lax.psum_scatter(
        (trans_dot(dpre, w_lin1) + ADAPT * exact_dot(up_part, a_lin1.T)).astype(jnp.bfloat16),
        "tensor",
        scatter_dimension=0,
        tiled=True,
    ).astype(jnp.float32)
    dmiddle = dout_f + norm_back(dxn2, normal_two, inv_two, gain_two)
    dya_local = (valid_local * dmiddle).astype(jnp.bfloat16)
    dya = lax.all_gather(dya_local, "tensor", axis=0, tiled=True)
    upp = trans_dot(dya, b_proj)
    datt = (trans_dot(dya, proj_weight) + ADAPT * exact_dot(upp, a_proj.T)).astype(jnp.bfloat16)
    grad_proj_up_t = ADAPT * cross_dot(down_p, dya)
    grad_proj_down_t = ADAPT * cross_dot(att, upp)
    dqueries, dkeys, dvalues = attention_back(
        queries, key_win, value_win, log_total, to_windows(datt), table_h, table_w
    )
    dqkv = jnp.stack(
        [from_windows(dqueries), from_windows(dkeys), from_windows(dvalues)], axis=1
    ).reshape(full_rows, -1)
    upq = trans_dot(dqkv, b_qkv)
    grad_qkv_up_t = (ADAPT * cross_dot(down_q, dqkv)).reshape(RANK, 3, -1)
    grad_qkv_down_t = ADAPT * cross_dot(xn1, upq)
    up_part = upq
    dxn1 = lax.psum_scatter(
        (trans_dot(dqkv, qkv_flat) + ADAPT * exact_dot(up_part, a_qkv.T)).astype(jnp.bfloat16),
        "tensor",
        scatter_dimension=0,
        tiled=True,
    ).astype(jnp.float32)
    grad_tokens = (dmiddle + norm_back(valid_local * dxn1, normal_one, inv_one, gain_one)).astype(
        jnp.bfloat16
    )
    grad_qkv_up, grad_proj_down, grad_lin1_up, grad_lin2_down = lax.psum(
        (
            into_slot(grad_qkv_up_t),
            into_slot(grad_proj_down_t),
            into_slot(grad_lin1_up_t),
            into_slot(grad_lin2_down_t),
        ),
        "dp",
    )
    grad_qkv_down, grad_proj_up, grad_lin1_down, grad_lin2_up = lax.psum(
        (
            into_slot(grad_qkv_down_t),
            into_slot(grad_proj_up_t),
            into_slot(grad_lin1_down_t),
            into_slot(grad_lin2_up_t),
        ),
        ("dp", "tensor"),
    )
    return (
        output,
        grad_tokens,
        grad_qkv_down,
        grad_qkv_up,
        grad_proj_down,
        grad_proj_up,
        grad_lin1_down,
        grad_lin1_up,
        grad_lin2_down,
        grad_lin2_up,
    )


def solution(mesh):
    placed = (
        P(("dp", "tensor"), None),
        P(("dp", "tensor"), None),
        P(),
        P(),
        P(),
        P(None, None, "tensor"),
        P(None, "tensor"),
        P(),
        P(),
        P("tensor", None),
        P(),
        P(),
        P(),
        P(None, "tensor"),
        P("tensor"),
        P("tensor", None),
        P(),
        P(),
        P(None, None, None, "tensor"),
        P(None, "tensor", None),
        P(),
        P(),
        P(None, None, "tensor"),
        P(None, "tensor", None),
        P(),
    )
    return jax.shard_map(
        on_device,
        mesh=mesh,
        in_specs=placed,
        out_specs=(
            P(("dp", "tensor"), None),
            P(("dp", "tensor"), None),
            P(),
            P(None, None, None, "tensor"),
            P(None, "tensor", None),
            P(),
            P(),
            P(None, None, "tensor"),
            P(None, "tensor", None),
            P(),
        ),
        check_vma=False,
    )
```

profile of v0, /device:TPU:0, one launch (start us, length us, event | category | flops | bytes accessed | tf_op | source)
XLA Modules:
  0.0 929.5 jit_solution(8334608292282891529)
XLA Ops:
  19.2 28.9 %all-gather.9.cloned.1.call-done = bf16[4,343,1280]{2,1,0:T(8,128)(2,1)} async-done(((bf16[1,343,1280]{2,1,0:T(8,128)(2,1)}), bf16[4,343,1280]{2,1,0:T(8,128)(2,1)}) %all-gather.9.cloned.1.call-update) | async-done | bytes 3512336 | tf_op jit(solution)/shard_map/all_gather | solution.py:205
  100.1 6.8 convolution_bitcast_fusion.2
  112.7 6.8 convolution_bitcast_fusion.1
  125.8 16.1 %add.258 = f32[7,4,14,14,14,14]{5,4,3,2,1,0:T(8,128)} broadcast(f32[7,4,14,14,14]{4,3,2,1,0:T(8,128)} %copy.105), dimensions={0,1,2,3,5} | broadcast | bytes 4609920 | tf_op jit(solution)/shard_map/add | solution.py:86
  141.9 26.9 %add.259 = f32[7,4,196,196]{3,2,1,0:T(8,128)} reshape(f32[7,4,14,14,14,14]{5,4,3,2,1,0:T(8,128)} %add.258) | data formatting | bytes 8605184 | tf_op jit(solution)/shard_map/add | solution.py:86
  168.8 6.8 copy.106
  175.6 16.6 %add.255 = f32[7,4,14,14,14,14]{5,4,3,2,1,0:T(8,128)} broadcast(f32[7,4,14,14,14]{4,3,2,1,0:T(8,128)} %copy.101), dimensions={0,1,2,3,4} | broadcast | bytes 4609920 | tf_op jit(solution)/shard_map/add | solution.py:86
  192.2 26.9 %add.256 = f32[7,4,196,196]{3,2,1,0:T(8,128)} reshape(f32[7,4,14,14,14,14]{5,4,3,2,1,0:T(8,128)} %add.255) | data formatting | bytes 8605184 | tf_op jit(solution)/shard_map/add | solution.py:86
  219.1 6.5 copy.102
  254.6 35.5 %fusion = bf16[344,1280]{1,0:T(8,128)(2,1)} fusion(bf16[1372,1280]{1,0:T(8,128)(2,1)} %fusion.13), kind=kCustom, calls=%all-reduce-scatter | all-reduce-scatter fusion | flops 1761281 | bytes 4393472
  306.8 33.4 %all-gather.13.cloned.1.call-done = bf16[4,343,1280]{2,1,0:T(8,128)(2,1)} async-done(((bf16[1,343,1280]{2,1,0:T(8,128)(2,1)}), bf16[4,343,1280]{2,1,0:T(8,128)(2,1)}) %all-gather.13.cloned.1.call-update) | async-done | bytes 3512336 | tf_op jit(solution)/shard_map/all_gather | solution.py:271
  348.1 9.0 fusion.152
  357.2 15.9 %all-gather.11.cloned.1.call-done = bf16[4,343,1280]{2,1,0:T(8,128)(2,1)} async-done(((bf16[1,343,1280]{2,1,0:T(8,128)(2,1)}), bf16[4,343,1280]{2,1,0:T(8,128)(2,1)}) %all-gather.11.cloned.1.call-update) | async-done | bytes 3512336 | tf_op jit(solution)/shard_map/all_gather | solution.py:242
  386.0 22.5 %multiply_convert_fusion = (bf16[1372,1280]{1,0:T(8,128)(2,1)}, f32[1372,1280]{1,0:T(8,128)S(1)}, f32[1372,1280]{1,0:T(8,128)}) fusion(f32[1372,1280]{1,0:T(8,128)S(1)} %convolution_add_fusion, f32[1372,16]{0,1:T(8,128)S(1)} %fusion.81, bf16[8,16,1280]{2,1,0:T(8,128)(2,1)} %param.47, s32[]{:T(128)S(6)} %select_n.86), kind=kOutput, calls=%fused_computation.21 | convolution fusion | flops 454845440 | bytes 24715012 | tf_op jit(solution)/shard_map/dot_general | solution.py:30
  408.5 9.7 %add_convert_fusion = bf16[1372,1280]{1,0:T(8,128)(2,1)S(1)} fusion(f32[1372,1280]{1,0:T(8,128)S(1)} %get-tuple-element.31, f32[1372,1280]{1,0:T(8,128)S(1)} %bitcast.198, f32[1372,16]{0,1:T(8,128)S(1)} %fusion.71, f32[1372,1280]{1,0:T(8,128)} %get-tuple-element.47, bf16[8,1280,16]{1,2,0:T(8,128)(2,1)} %param.48, s32[]{:T(128)S(6)} %select_n.86), kind=kOutput, calls=%fused_computation.20 | convolution fusion | flops 365281280 | bytes 24735492 | tf_op jit(solution)/shard_map/dot_general | solution.py:30
  430.9 35.2 %fusion.2 = bf16[344,1280]{1,0:T(8,128)(2,1)} fusion(bf16[1372,1280]{1,0:T(8,128)(2,1)} %fusion.11), kind=kCustom, calls=%all-reduce-scatter.2 | all-reduce-scatter fusion | flops 1761281 | bytes 4393472
  469.0 6.7 concatenate.2
  502.1 6.5 fusion.12
  508.5 9.3 all-gather.15.cloned.1.call-done
  588.3 26.1 %reshape.202 = f32[7,4,14,14,14,14]{5,4,3,2,1,0:T(8,128)} reshape(f32[7,4,196,196]{3,2,1,0:T(8,128)} %copy.117) | data formatting | bytes 8605184 | tf_op jit(solution)/shard_map/reshape | solution.py:121
  614.4 19.9 %fusion.144 = (f32[7,4,14,14,14]{4,3,2,1,0:T(8,128)}, f32[7,4,14,14,14]{4,3,2,1,0:T(8,128)}) fusion(f32[7,4,14,14,14,14]{5,4,3,2,1,0:T(8,128)} %reshape.202), kind=kLoop, calls=%fused_computation.232 | loop fusion | flops 1997632 | bytes 4917248 | tf_op jit(solution)/shard_map/reduce_sum | solution.py:123
  678.7 68.8 %fusion.145 = (bf16[344,1280]{1,0:T(8,128)(2,1)}, bf16[344,1280]{1,0:T(8,128)(2,1)}) fusion(bf16[1372,1280]{1,0:T(8,128)(2,1)} %fusion.12, bf16[1372,1280]{1,0:T(8,128)(2,1)} %fusion.10), kind=kCustom, calls=%all-reduce-scatter.4 | all-reduce-scatter fusion | flops 3522561 | bytes 8786432
  773.5 31.3 %all-reduce.14.cloned.1.call-done = (f32[8,1280,16]{1,2,0:T(8,128)}, f32[8,16,1280]{2,1,0:T(8,128)}, f32[8,1280,16]{1,2,0:T(8,128)}, f32[8,16,1280]{2,1,0:T(8,128)}) async-done(((f32[8,1280,16]{1,2,0:T(8,128)}, f32[8,16,1280]{2,1,0:T(8,128)}, f32[8,1280,16]{1,2,0:T(8,128)}, f32[8,16,1280]{2,1,0:T(8,128)}), (f32[8,1280,16]{1,2,0:T(8,128)}, f32[8,16,1280]{2,1,0:T(8,128)}, f32[8,1280,16]{1,2,0:T(8,128)}, ...) | async-done | bytes 2621456 | tf_op jit(solution)/shard_map/psum | solution.py:322
  804.8 107.7 %all-reduce.16.cloned.1.call-done = (f32[8,16,3,320]{3,1,2,0:T(8,128)}, f32[8,320,16]{1,2,0:T(8,128)}, f32[8,16,1280]{2,1,0:T(8,128)}, f32[8,1280,16]{1,2,0:T(8,128)}) async-done(((f32[8,16,3,320]{3,1,2,0:T(8,128)}, f32[8,320,16]{1,2,0:T(8,128)}, f32[8,16,1280]{2,1,0:T(8,128)}, f32[8,1280,16]{1,2,0:T(8,128)}), (f32[8,16,3,320]{3,1,2,0:T(8,128)}, f32[8,320,16]{1,2,0:T(8,128)}, f32[8,16,1280]{2,1,0:T(8,128)}, ...) | async-done | bytes 1966096 | tf_op jit(solution)/shard_map/psum | solution.py:313
  (300 shorter events, 331.8 us)
Async XLA Ops:
  7.2 373.8 %copy-start = (bf16[1280,1280]{1,0:T(8,128)(2,1)S(1)}, bf16[1280,1280]{1,0:T(8,128)(2,1)}, u32[]{:S(2)}) copy-start(bf16[1280,1280]{1,0:T(8,128)(2,1)} %param.38) | copy-start | bytes 9830404
  7.2 40.8 %all-gather.9.cloned.1.call-start = ((), (), s32[]{:S(2)}) async-start(), calls=%async_computation | async-start | bytes 4403200 | tf_op jit(solution)/shard_map/all_gather | solution.py:205
  14.5 325.7 %all-gather.13.cloned.1.call-start = ((), (), s32[]{:S(2)}) async-start(), calls=%async_computation.2 | async-start | bytes 4403200 | tf_op jit(solution)/shard_map/all_gather | solution.py:271
  18.3 43.4 %copy-start.45 = (bf16[16,960]{1,0:T(8,128)(2,1)}, bf16[16,960]{1,0:T(8,128)(2,1)S(1)}, u32[]{:S(2)}) copy-start(bf16[16,960]{1,0:T(8,128)(2,1)S(1)} %reshape.189) | copy-start | bytes 92164
  18.7 93.9 %copy-start.40 = (bf16[14,14,80,1,1]{2,1,0,3,4:T(8,128)(2,1)}, bf16[14,14,80,1,1]{2,1,0,3,4:T(8,128)(2,1)S(1)}, u32[]{:S(2)}) copy-start(bf16[14,14,80,1,1]{2,1,0,3,4:T(8,128)(2,1)S(1)} %reshape.212) | copy-start | bytes 94084
  19.2 80.9 %copy-start.42 = (bf16[14,14,80,1,1]{2,1,0,3,4:T(8,128)(2,1)}, bf16[14,14,80,1,1]{2,1,0,3,4:T(8,128)(2,1)S(1)}, u32[]{:S(2)}) copy-start(bf16[14,14,80,1,1]{2,1,0,3,4:T(8,128)(2,1)S(1)} %reshape.211) | copy-start | bytes 94084
  254.6 37.5 %copy-start.53 = (bf16[1280]{0:T(1024)(128)(2,1)S(1)}, bf16[1280]{0:T(1024)(128)(2,1)}, u32[]{:S(2)}) copy-start(bf16[1280]{0:T(1024)(128)(2,1)} %param.35) | copy-start | bytes 7684
  254.6 37.6 %copy-start.54 = (bf16[1280]{0:T(1024)(128)(2,1)S(1)}, bf16[1280]{0:T(1024)(128)(2,1)}, u32[]{:S(2)}) copy-start(bf16[1280]{0:T(1024)(128)(2,1)} %param.36) | copy-start | bytes 7684
  254.6 37.6 %copy-start.55 = (bf16[1280]{0:T(1024)(128)(2,1)S(1)}, bf16[1280]{0:T(1024)(128)(2,1)}, u32[]{:S(2)}) copy-start(bf16[1280]{0:T(1024)(128)(2,1)} %param.37) | copy-start | bytes 7684
  254.6 37.6 %copy-start.59 = (u32[32]{0:T(128)S(1)}, u32[32]{0:T(128)}, u32[]{:S(2)}) copy-start(u32[32]{0:T(128)} %constant.209) | copy-start | bytes 388
  290.8 2.6 collective-permute-start
  306.0 67.1 %all-gather.11.cloned.1.call-start = ((), (), s32[]{:S(2)}) async-start(), calls=%async_computation.1 | async-start | bytes 4403200 | tf_op jit(solution)/shard_map/all_gather | solution.py:242
  306.7 211.1 %all-gather.15.cloned.1.call-start = ((), (), s32[]{:S(2)}) async-start(), calls=%async_computation.3 | async-start | bytes 4403200 | tf_op jit(solution)/shard_map/all_gather | solution.py:289
  348.1 60.4 %copy-start.37 = (f32[1372,16]{0,1:T(8,128)}, f32[1372,16]{0,1:T(8,128)S(1)}, u32[]{:S(2)}) copy-start(f32[1372,16]{0,1:T(8,128)S(1)} %fusion.71) | copy-start | bytes 263428
  381.1 27.4 %slice-start.2 = ((s8[7045120]{0:T(1024)(128)(4,1)}), s8[4194304]{0:T(1024)(128)(4,1)S(1)}, s32[]{:S(2)}) async-start(s8[7045120]{0:T(1024)(128)(4,1)} %bitcast.197), calls=%async_computation.8 | async-start | bytes 8388608
  386.0 22.5 %slice-start.3 = ((s8[7045120]{0:T(1024)(128)(4,1)}), s8[2850816]{0:T(1024)(128)(4,1)S(1)}, s32[]{:S(2)}) async-start(s8[7045120]{0:T(1024)(128)(4,1)} %bitcast.197), calls=%async_computation.9 | async-start | bytes 5701632
  466.8 2.2 collective-permute-start.2
  483.1 321.8 %all-reduce.14.cloned.1.call-start = ((), (), s32[]{:S(2)}) async-start(), calls=%async_computation.4 | async-start | bytes 5242880 | tf_op jit(solution)/shard_map/psum | solution.py:322
  614.4 19.9 %copy-start.41 = (bf16[14,14,80,1,1]{2,1,0,3,4:T(8,128)(2,1)S(1)}, bf16[14,14,80,1,1]{2,1,0,3,4:T(8,128)(2,1)}, u32[]{:S(2)}) copy-start(bf16[14,14,80,1,1]{2,1,0,3,4:T(8,128)(2,1)} %copy-done.40) | copy-start | bytes 94084
  666.3 246.2 %all-reduce.16.cloned.1.call-start = ((), (), s32[]{:S(2)}) async-start(), calls=%async_computation.5 | async-start | bytes 4194304 | tf_op jit(solution)/shard_map/psum | solution.py:313
  678.7 74.8 %copy-start.57 = (bf16[1280]{0:T(1024)(128)(2,1)S(1)}, bf16[1280]{0:T(1024)(128)(2,1)}, u32[]{:S(2)}) copy-start(bf16[1280]{0:T(1024)(128)(2,1)} %param.41) | copy-start | bytes 7684
  747.5 18.1 %copy-start.52 = (f32[343]{0:T(512)S(1)}, f32[343]{0:T(512)}, u32[]{:S(2)}) copy-start(f32[343]{0:T(512)} %copy-done.51) | copy-start | bytes 4120
  748.3 5.2 collective-permute-start.3
  750.3 9.2 collective-permute-start.1
  (54 other events, 293.1 us)
Sparse Core Ops, SparseCore 0:
  14.7 33.3 all-gather.8
  306.1 34.0 all-gather.12
  342.4 30.6 all-gather.10
  483.2 34.5 all-gather.14
  666.4 138.3 all-reduce.13
  810.3 102.1 all-reduce.15
where the time goes:
time: 941 us; the launch traced here: 930 us
  local copies, waits for them, and re-layouts  291 us (31%)
  waiting for transfers between devices  228 us (24%)
  matrix products  184 us (20%)
  blocking collectives  140 us (15%)
  other arithmetic  61.4 us (7%)
  between operations  17.9 us (2%)
    unnamed x3, blocking collectives  140 us
    psum x1, waiting for transfers between devices, on_device(): lax.psum((into_slot(grad_qkv_up_t), into_slot(grad_proj_down_t), into_slo...  108 us
    add x6, local copies, waits for them, and re-layouts, window_scores(): base_scores.reshape(win_count, head_count, WIN, WIN, WIN, WIN)  99.8 us
    unnamed x160, local copies, waits for them, and re-layouts  66.6 us
    dot_general x10, matrix products, exact_dot(): return jnp.dot(first_op, second_op.astype(jnp.float32), precision=HIGH)  62.1 us
    all_gather x1, waiting for transfers between devices, on_device(): dy2 = lax.all_gather(dy2_local, 'tensor', axis=0, tiled=True)  33.4 us
    reshape x2, local copies, waits for them, and re-layouts, attention_back(): dscore.astype(jnp.float32)  31.3 us
    psum x1, waiting for transfers between devices, on_device(): lax.psum((into_slot(grad_qkv_down_t), into_slot(grad_proj_up_t), into_slo...  31.3 us
  transfers between devices with their start and end apart: 10, of which 7 were waited for; matrix products, arithmetic and copies ran while one was open for 16% of the time, Pallas kernels for 0%

commit v1 on v0

--- a/solution.py
+++ b/solution.py
@@ -14,6 +14,12 @@
 HIGH = lax.Precision.HIGHEST
 ADAPT = 0.5
 EPS = 1e-06
+
+
+def in_order(blocks, dim):
+    dims = list(blocks.shape[1:])
+    dims[dim] *= blocks.shape[0]
+    return jnp.moveaxis(blocks, 0, dim).reshape(dims)
 
 
 def fast_dot(first_op, second_op):
@@ -202,7 +208,14 @@
     xn1_local = (valid_local * (normal_one * gain_one + norm1_shift.astype(jnp.float32))).astype(
         jnp.bfloat16
     )
-    xn1 = lax.all_gather(xn1_local, "tensor", axis=0, tiled=True)
+    size = lax.axis_size("tensor")
+    right = [(i, (i + 1) % size) for i in range(size)]
+    blocks = [xn1_local]
+    while len(blocks) < size:
+        blocks.append(lax.ppermute(blocks[-1], "tensor", right))
+    position_2 = lax.axis_index("tensor")
+    blocks = jnp.stack(blocks)[(position_2 - jnp.arange(size)) % size]
+    xn1 = in_order(blocks, 0)
     down_q = fast_dot(xn1, a_qkv)
     qkv = (
         fast_dot(xn1, qkv_flat)

time: 941 us -> 950 us (level)
    ppermute x0 -> x3, waiting for transfers between devices: none -> 31.9 us  [on_device(): blocks.append(lax.ppermute(blocks[-1], 'tensor', right))]
    all_gather x1 -> x0, waiting for transfers between devices: 28.9 us -> none  [on_device(): xn1 = lax.all_gather(xn1_local, 'tensor', axis=0, tiled=True)]
    unnamed x160 -> x159, local copies, waits for them, and re-layouts: 66.6 us -> 61.7 us
  transfers between devices with their start and end apart: 10 -> 12, of which waited for: 7 -> 9; matrix products, arithmetic and copies ran while one was open for 16% -> 16% of each run, Pallas kernels for 0% -> 0%
where the time goes in v1:
time: 950 us; the launch traced here: 942 us
  local copies, waits for them, and re-layouts  295 us (31%)
  waiting for transfers between devices  231 us (24%)
  matrix products  184 us (19%)
  blocking collectives  140 us (15%)
  other arithmetic  66 us (7%)
  between operations  17.5 us (2%)
    unnamed x3, blocking collectives  140 us
    psum x1, waiting for transfers between devices, on_device(): lax.psum((into_slot(grad_qkv_up_t), into_slot(grad_proj_down_t), into_slo...  108 us
    add x6, local copies, waits for them, and re-layouts, window_scores(): base_scores.reshape(win_count, head_count, WIN, WIN, WIN, WIN)  99.7 us
    dot_general x10, matrix products, exact_dot(): return jnp.dot(first_op, second_op.astype(jnp.float32), precision=HIGH)  61.7 us
    unnamed x159, local copies, waits for them, and re-layouts  61.7 us
    all_gather x1, waiting for transfers between devices, on_device(): dy2 = lax.all_gather(dy2_local, 'tensor', axis=0, tiled=True)  33.8 us
    ppermute x3, waiting for transfers between devices, on_device(): blocks.append(lax.ppermute(blocks[-1], 'tensor', right))  31.9 us
    reshape x2, local copies, waits for them, and re-layouts, attention_back(): dscore.astype(jnp.float32)  31.3 us
  transfers between devices with their start and end apart: 12, of which 9 were waited for; matrix products, arithmetic and copies ran while one was open for 16% of the time, Pallas kernels for 0%

profile of v1, /device:TPU:0, one launch (start us, length us, event | category | flops | bytes accessed | tf_op | source)
XLA Modules:
  0.0 942.2 jit_solution(11182303753271264866)
XLA Ops:
  14.1 12.7 %collective-permute-done = bf16[343,1280]{1,0:T(8,128)(2,1)} collective-permute-done((bf16[343,1280]{1,0:T(8,128)(2,1)S(1)}, bf16[343,1280]{1,0:T(8,128)(2,1)}, u32[]{:S(2)}, u32[]{:S(2)}) %collective-permute-start) | collective-permute-done | bytes 878112 | tf_op jit(solution)/shard_map/ppermute | solution.py:215
  31.0 8.6 collective-permute-done.1
  41.8 10.6 %collective-permute-done.2 = bf16[343,1280]{1,0:T(8,128)(2,1)} collective-permute-done((bf16[343,1280]{1,0:T(8,128)(2,1)}, bf16[343,1280]{1,0:T(8,128)(2,1)}, u32[]{:S(2)}, u32[]{:S(2)}) %collective-permute-start.2) | collective-permute-done | bytes 878112 | tf_op jit(solution)/shard_map/ppermute | solution.py:215
  112.5 6.8 convolution_bitcast_fusion.2
  125.0 6.8 convolution_bitcast_fusion.1
  138.2 16.1 %add.283 = f32[7,4,14,14,14,14]{5,4,3,2,1,0:T(8,128)} broadcast(f32[7,4,14,14,14]{4,3,2,1,0:T(8,128)} %copy.105), dimensions={0,1,2,3,5} | broadcast | bytes 4609920 | tf_op jit(solution)/shard_map/add | solution.py:92
  154.3 26.9 %add.284 = f32[7,4,196,196]{3,2,1,0:T(8,128)} reshape(f32[7,4,14,14,14,14]{5,4,3,2,1,0:T(8,128)} %add.283) | data formatting | bytes 8605184 | tf_op jit(solution)/shard_map/add | solution.py:92
  187.6 16.6 %add.280 = f32[7,4,14,14,14,14]{5,4,3,2,1,0:T(8,128)} broadcast(f32[7,4,14,14,14]{4,3,2,1,0:T(8,128)} %copy.101), dimensions={0,1,2,3,4} | broadcast | bytes 4609920 | tf_op jit(solution)/shard_map/add | solution.py:92
  204.2 26.9 %add.281 = f32[7,4,196,196]{3,2,1,0:T(8,128)} reshape(f32[7,4,14,14,14,14]{5,4,3,2,1,0:T(8,128)} %add.280) | data formatting | bytes 8605184 | tf_op jit(solution)/shard_map/add | solution.py:92
  231.0 6.9 copy.102
  267.0 35.7 %fusion = bf16[344,1280]{1,0:T(8,128)(2,1)} fusion(bf16[1372,1280]{1,0:T(8,128)(2,1)} %fusion.13), kind=kCustom, calls=%all-reduce-scatter | all-reduce-scatter fusion | flops 1761281 | bytes 4393472
  319.4 33.8 %all-gather.9.cloned.1.call-done = bf16[4,343,1280]{2,1,0:T(8,128)(2,1)} async-done(((bf16[1,343,1280]{2,1,0:T(8,128)(2,1)}), bf16[4,343,1280]{2,1,0:T(8,128)(2,1)}) %all-gather.9.cloned.1.call-update) | async-done | bytes 3512336 | tf_op jit(solution)/shard_map/all_gather | solution.py:284
  361.1 9.2 fusion.153
  370.3 15.8 %all-gather.7.cloned.1.call-done = bf16[4,343,1280]{2,1,0:T(8,128)(2,1)} async-done(((bf16[1,343,1280]{2,1,0:T(8,128)(2,1)}), bf16[4,343,1280]{2,1,0:T(8,128)(2,1)}) %all-gather.7.cloned.1.call-update) | async-done | bytes 3512336 | tf_op jit(solution)/shard_map/all_gather | solution.py:255
  398.9 22.5 %multiply_convert_fusion = (bf16[1372,1280]{1,0:T(8,128)(2,1)}, f32[1372,1280]{1,0:T(8,128)S(1)}, f32[1372,1280]{1,0:T(8,128)}) fusion(f32[1372,1280]{1,0:T(8,128)S(1)} %convolution_add_fusion, f32[1372,16]{0,1:T(8,128)S(1)} %fusion.80, bf16[8,16,1280]{2,1,0:T(8,128)(2,1)} %param.47, s32[]{:T(128)S(6)} %select_n.111), kind=kOutput, calls=%fused_computation.22 | convolution fusion | flops 454845440 | bytes 24715012 | tf_op jit(solution)/shard_map/dot_general | solution.py:36
  421.5 9.5 %add_convert_fusion = bf16[1372,1280]{1,0:T(8,128)(2,1)S(1)} fusion(f32[1372,1280]{1,0:T(8,128)S(1)} %get-tuple-element.31, f32[1372,1280]{1,0:T(8,128)S(1)} %bitcast.203, f32[1372,16]{0,1:T(8,128)S(1)} %fusion.70, f32[1372,1280]{1,0:T(8,128)} %get-tuple-element.47, bf16[8,1280,16]{1,2,0:T(8,128)(2,1)} %param.48, s32[]{:T(128)S(6)} %select_n.111), kind=kOutput, calls=%fused_computation.21 | convolution fusion | flops 365281280 | bytes 24735492 | tf_op jit(solution)/shard_map/dot_general | solution.py:36
  443.6 35.2 %fusion.2 = bf16[344,1280]{1,0:T(8,128)(2,1)} fusion(bf16[1372,1280]{1,0:T(8,128)(2,1)} %fusion.11), kind=kCustom, calls=%all-reduce-scatter.2 | all-reduce-scatter fusion | flops 1761281 | bytes 4393472
  481.8 6.7 concatenate.2
  521.2 9.3 all-gather.11.cloned.1.call-done
  601.1 26.1 %reshape.255 = f32[7,4,14,14,14,14]{5,4,3,2,1,0:T(8,128)} reshape(f32[7,4,196,196]{3,2,1,0:T(8,128)} %copy.117) | data formatting | bytes 8605184 | tf_op jit(solution)/shard_map/reshape | solution.py:127
  627.2 20.1 %fusion.145 = (f32[7,4,14,14,14]{4,3,2,1,0:T(8,128)}, f32[7,4,14,14,14]{4,3,2,1,0:T(8,128)}) fusion(f32[7,4,14,14,14,14]{5,4,3,2,1,0:T(8,128)} %reshape.255), kind=kLoop, calls=%fused_computation.240 | loop fusion | flops 1997632 | bytes 4917248 | tf_op jit(solution)/shard_map/reduce_sum | solution.py:129
  691.7 68.9 %fusion.146 = (bf16[344,1280]{1,0:T(8,128)(2,1)}, bf16[344,1280]{1,0:T(8,128)(2,1)}) fusion(bf16[1372,1280]{1,0:T(8,128)(2,1)} %fusion.12, bf16[1372,1280]{1,0:T(8,128)(2,1)} %fusion.10), kind=kCustom, calls=%all-reduce-scatter.4 | all-reduce-scatter fusion | flops 3522561 | bytes 8786432
  786.6 31.3 %all-reduce.14.cloned.1.call-done = (f32[8,1280,16]{1,2,0:T(8,128)}, f32[8,16,1280]{2,1,0:T(8,128)}, f32[8,1280,16]{1,2,0:T(8,128)}, f32[8,16,1280]{2,1,0:T(8,128)}) async-done(((f32[8,1280,16]{1,2,0:T(8,128)}, f32[8,16,1280]{2,1,0:T(8,128)}, f32[8,1280,16]{1,2,0:T(8,128)}, f32[8,16,1280]{2,1,0:T(8,128)}), (f32[8,1280,16]{1,2,0:T(8,128)}, f32[8,16,1280]{2,1,0:T(8,128)}, f32[8,1280,16]{1,2,0:T(8,128)}, ...) | async-done | bytes 2621456 | tf_op jit(solution)/shard_map/psum | solution.py:335
  817.8 107.7 %all-reduce.16.cloned.1.call-done = (f32[8,16,3,320]{3,1,2,0:T(8,128)}, f32[8,320,16]{1,2,0:T(8,128)}, f32[8,16,1280]{2,1,0:T(8,128)}, f32[8,1280,16]{1,2,0:T(8,128)}) async-done(((f32[8,16,3,320]{3,1,2,0:T(8,128)}, f32[8,320,16]{1,2,0:T(8,128)}, f32[8,16,1280]{2,1,0:T(8,128)}, f32[8,1280,16]{1,2,0:T(8,128)}), (f32[8,16,3,320]{3,1,2,0:T(8,128)}, f32[8,320,16]{1,2,0:T(8,128)}, f32[8,16,1280]{2,1,0:T(8,128)}, ...) | async-done | bytes 1966096 | tf_op jit(solution)/shard_map/psum | solution.py:326
  (308 shorter events, 354.0 us)
Async XLA Ops:
  7.2 386.8 %copy-start = (bf16[1280,1280]{1,0:T(8,128)(2,1)S(1)}, bf16[1280,1280]{1,0:T(8,128)(2,1)}, u32[]{:S(2)}) copy-start(bf16[1280,1280]{1,0:T(8,128)(2,1)} %param.38) | copy-start | bytes 9830404
  7.2 346.0 %all-gather.9.cloned.1.call-start = ((), (), s32[]{:S(2)}) async-start(), calls=%async_computation.1 | async-start | bytes 4403200 | tf_op jit(solution)/shard_map/all_gather | solution.py:284
  8.8 47.0 %copy-start.49 = (f32[343]{0:T(512)}, f32[343]{0:T(512)S(1)}, u32[]{:S(2)}) copy-start(f32[343]{0:T(512)S(1)} %broadcast_multiply_fusion.13) | copy-start | bytes 4120
  10.4 45.5 %copy-start.51 = (f32[343]{0:T(512)}, f32[343]{0:T(512)S(1)}, u32[]{:S(2)}) copy-start(f32[343]{0:T(512)S(1)} %add_rsqrt_fusion.1) | copy-start | bytes 4120
  11.1 44.8 %copy-start.47 = (f32[1280]{0:T(1024)}, f32[1280]{0:T(1024)S(1)}, u32[]{:S(2)}) copy-start(f32[1280]{0:T(1024)S(1)} %convert_element_type.157) | copy-start | bytes 15364
  13.6 13.2 %collective-permute-start = (bf16[343,1280]{1,0:T(8,128)(2,1)S(1)}, bf16[343,1280]{1,0:T(8,128)(2,1)}, u32[]{:S(2)}, u32[]{:S(2)}) collective-permute-start(bf16[343,1280]{1,0:T(8,128)(2,1)S(1)} %fusion.40), channel_id=1, source_target_pairs={{0,1},{1,2},{2,3},{3,0},{4,5},{5,6},{6,7},{7,4},{8,9},{9,10},{10,1... | collective-permute-start | bytes 2634248 | tf_op jit(solution)/shard_map/ppermute | solution.py:215
  26.9 12.7 %collective-permute-start.1 = (bf16[343,1280]{1,0:T(8,128)(2,1)}, bf16[343,1280]{1,0:T(8,128)(2,1)}, u32[]{:S(2)}, u32[]{:S(2)}) collective-permute-start(bf16[343,1280]{1,0:T(8,128)(2,1)} %collective-permute-done), channel_id=1, source_target_pairs={{0,1},{1,2},{2,3},{3,0},{4,5},{5,6},{6,7},{7,4},{8,9},{9,10},{10,1... | collective-permute-start | bytes 2634248 | tf_op jit(solution)/shard_map/ppermute | solution.py:215
  30.5 43.5 %copy-start.45 = (bf16[16,960]{1,0:T(8,128)(2,1)}, bf16[16,960]{1,0:T(8,128)(2,1)S(1)}, u32[]{:S(2)}) copy-start(bf16[16,960]{1,0:T(8,128)(2,1)S(1)} %reshape.242) | copy-start | bytes 92164
  31.0 94.1 %copy-start.40 = (bf16[14,14,80,1,1]{2,1,0,3,4:T(8,128)(2,1)}, bf16[14,14,80,1,1]{2,1,0,3,4:T(8,128)(2,1)S(1)}, u32[]{:S(2)}) copy-start(bf16[14,14,80,1,1]{2,1,0,3,4:T(8,128)(2,1)S(1)} %reshape.271) | copy-start | bytes 94084
  39.6 12.7 %collective-permute-start.2 = (bf16[343,1280]{1,0:T(8,128)(2,1)}, bf16[343,1280]{1,0:T(8,128)(2,1)}, u32[]{:S(2)}, u32[]{:S(2)}) collective-permute-start(bf16[343,1280]{1,0:T(8,128)(2,1)} %collective-permute-done.1), channel_id=1, source_target_pairs={{0,1},{1,2},{2,3},{3,0},{4,5},{5,6},{6,7},{7,4},{8,9},{9,10},{10,1... | collective-permute-start | bytes 2634248 | tf_op jit(solution)/shard_map/ppermute | solution.py:215
  40.0 72.4 %copy-start.42 = (bf16[14,14,80,1,1]{2,1,0,3,4:T(8,128)(2,1)}, bf16[14,14,80,1,1]{2,1,0,3,4:T(8,128)(2,1)S(1)}, u32[]{:S(2)}) copy-start(bf16[14,14,80,1,1]{2,1,0,3,4:T(8,128)(2,1)S(1)} %reshape.270) | copy-start | bytes 94084
  267.0 37.8 %copy-start.54 = (bf16[1280]{0:T(1024)(128)(2,1)S(1)}, bf16[1280]{0:T(1024)(128)(2,1)}, u32[]{:S(2)}) copy-start(bf16[1280]{0:T(1024)(128)(2,1)} %param.36) | copy-start | bytes 7684
  267.0 37.8 %copy-start.55 = (bf16[1280]{0:T(1024)(128)(2,1)S(1)}, bf16[1280]{0:T(1024)(128)(2,1)}, u32[]{:S(2)}) copy-start(bf16[1280]{0:T(1024)(128)(2,1)} %param.37) | copy-start | bytes 7684
  267.0 37.8 %copy-start.59 = (u32[32]{0:T(128)S(1)}, u32[32]{0:T(128)}, u32[]{:S(2)}) copy-start(u32[32]{0:T(128)} %constant.219) | copy-start | bytes 388
  303.5 2.6 collective-permute-start.3
  318.6 67.4 %all-gather.7.cloned.1.call-start = ((), (), s32[]{:S(2)}) async-start(), calls=%async_computation | async-start | bytes 4403200 | tf_op jit(solution)/shard_map/all_gather | solution.py:255
  319.4 211.2 %all-gather.11.cloned.1.call-start = ((), (), s32[]{:S(2)}) async-start(), calls=%async_computation.2 | async-start | bytes 4403200 | tf_op jit(solution)/shard_map/all_gather | solution.py:302
  361.1 60.4 %copy-start.37 = (f32[1372,16]{0,1:T(8,128)}, f32[1372,16]{0,1:T(8,128)S(1)}, u32[]{:S(2)}) copy-start(f32[1372,16]{0,1:T(8,128)S(1)} %fusion.70) | copy-start | bytes 263428
  479.5 2.2 collective-permute-start.5
  495.8 322.0 %all-reduce.14.cloned.1.call-start = ((), (), s32[]{:S(2)}) async-start(), calls=%async_computation.3 | async-start | bytes 5242880 | tf_op jit(solution)/shard_map/psum | solution.py:335
  679.3 246.2 %all-reduce.16.cloned.1.call-start = ((), (), s32[]{:S(2)}) async-start(), calls=%async_computation.4 | async-start | bytes 4194304 | tf_op jit(solution)/shard_map/psum | solution.py:326
  691.6 74.8 %copy-start.57 = (bf16[1280]{0:T(1024)(128)(2,1)S(1)}, bf16[1280]{0:T(1024)(128)(2,1)}, u32[]{:S(2)}) copy-start(bf16[1280]{0:T(1024)(128)(2,1)} %param.41) | copy-start | bytes 7684
  761.3 5.2 collective-permute-start.6
  763.3 9.2 collective-permute-start.4
  (56 other events, 454.7 us)
Sparse Core Ops, SparseCore 0:
  318.7 34.4 all-gather.8
  355.4 30.6 all-gather.6
  495.9 34.5 all-gather.10
  679.4 138.3 all-reduce.13
  823.3 102.1 all-reduce.15
